TPU v7x, 256 devices: a whole 4x4x8 slice. The times are simulated.
256 devices in a mesh: leaf: 128 (over y, x, z), rhs: 2 (over core).
Axes of the slice: x: 4, y: 4, z: 8, core: 2. Of those that a mesh axis runs over, the one named last changes fastest.
Arguments:
- values: bfloat16 [64, 1048576], P('rhs', 'leaf'), may hold values from -6 to 6
- points: float32 [3, 1048576], P(None, 'leaf'), may hold values from 0 to 1
- basis: bfloat16 [4096, 64, 256], P('leaf', 'rhs'), may hold values from -0.375 to 0.375
- near_list: int32 [4096, 9], P('leaf'), may hold values from 0 to 4095, as said below
- far_list: int32 [4096, 8], P('leaf'), may hold values from 0 to 4095, as said below
- far_count: int32 [4096], P('leaf'), may hold values from 1 to 8, as said below
- leaf_couple: bfloat16 [4096, 8, 64, 64], P('leaf'), may hold values from -0.25 to 0.25
- local_transfer: bfloat16 [2, 64, 64], replicated, may hold values from -0.75 to 0.75
- upper_transfer: bfloat16 [7, 2, 64, 64], replicated, may hold values from -0.75 to 0.75
- upper_couple: bfloat16 [7, 2, 64, 64], replicated, may hold values from -0.0234375 to 0.0234375
Outputs:
- potential: float32 [64, 1048576], P('rhs', 'leaf')
Inputs may be any that keep to these rules, and one draw needn't show every extreme that they name: `near_list`: row i holds leaf indices within 4 of i; its first entry is i and its last lies exactly 4 away unless the end of the leaves cuts it. `far_list`: row i holds leaf indices within 4 of i; its last entry lies exactly 4 away unless the end of the leaves cuts it. `far_count`: some leaf uses all 8 slots.
All inputs are finite; a program needn't handle non-finite values.
Results may differ from a plain program's by a relative error of at most 0.02.
Values may be sent and summed in bfloat16 or wider, within the bound.
A program may use at most 64 MiB of HBM per device.

v0:
```python
import math

import jax
import jax.numpy as jnp
from jax import lax
from jax.sharding import PartitionSpec as P

HW = 4


WAVE = 20.0
SMOOTH = 0.05


def extended(block, sides, width):
    for axis, dim in sides:
        count = lax.axis_size(axis)
        forward = [(i, i + 1) for i in range(count - 1)]
        backward = [(target, source) for source, target in forward]
        low = lax.ppermute(
            lax.slice_in_dim(block, block.shape[dim] - width, None, axis=dim), axis, forward
        )
        high = lax.ppermute(lax.slice_in_dim(block, 0, width, axis=dim), axis, backward)
        block = jnp.concatenate([low, block, high], axis=dim)
    return block


def kernel_block(targets, sources):
    gap_x = targets[0][:, None, :, None] - sources[0][:, :, None, :]
    gap_y = targets[1][:, None, :, None] - sources[1][:, :, None, :]
    gap_z = targets[2][:, None, :, None] - sources[2][:, :, None, :]
    squared = gap_x * gap_x + gap_y * gap_y + gap_z * gap_z
    factor = 1.0 / math.sqrt(sources.shape[2] * sources.shape[3])
    return (
        factor * jnp.cos(WAVE * jnp.sqrt(squared)) / jnp.sqrt(squared + SMOOTH * SMOOTH)
    ).astype(jnp.bfloat16)


def upward(level, transfer):
    pairs = level.reshape(level.shape[0] // 2, 2, level.shape[1], level.shape[2])
    return jnp.einsum("jsrk,skl->jrl", pairs, transfer, preferred_element_type=jnp.float32).astype(
        jnp.bfloat16
    )


def near_field(own_points, near_index, rim_points, rim_values, count):
    group = min(count, 4)

    def near_block(start):
        targets = lax.dynamic_slice_in_dim(own_points, start, group, 1)
        index = lax.dynamic_slice_in_dim(near_index, start, group, 0)
        kernel = kernel_block(targets, rim_points[:, index])
        return jnp.einsum(
            "gnpq,rgnq->rgp", kernel, rim_values[:, index], preferred_element_type=jnp.float32
        )

    starts = jnp.arange(count // group, dtype=jnp.int32) * group
    blocks = lax.map(near_block, starts)
    return jnp.transpose(blocks, (1, 0, 2, 3)).reshape(
        rim_values.shape[0], count, own_points.shape[2]
    )


def on_device(
    values,
    points,
    basis,
    near_list,
    far_list,
    far_count,
    leaf_couple,
    local_transfer,
    upper_transfer,
    upper_couple,
):
    leaf_dev = basis.shape[0]
    leaf_size = basis.shape[2]
    columns = values.shape[0]
    upper_levels = upper_transfer.shape[0]
    device = lax.axis_index("leaf")
    full_basis = lax.all_gather(basis, "rhs", axis=1, tiled=True)
    rank = full_basis.shape[1]
    grouped = values.reshape(columns, leaf_dev, leaf_size)
    leaf_coeff = jnp.einsum(
        "ikp,rip->irk", full_basis, grouped, preferred_element_type=jnp.float32
    ).astype(jnp.bfloat16)
    local_levels = leaf_dev.bit_length() - 1
    level = leaf_coeff
    for step in range(local_levels):
        level = upward(level, local_transfer)
    siblings = []
    nodes = lax.all_gather(level, "leaf", axis=0, tiled=True)
    for step in range(upper_levels):
        here = device // 2**step
        partner = here + 1 - 2 * (here % 2)
        siblings.append(lax.dynamic_index_in_dim(nodes, partner, 0, keepdims=False))
        if step < upper_levels - 1:
            nodes = upward(nodes, upper_transfer[step])
    local = None
    for step in reversed(range(upper_levels)):
        side = device // 2**step % 2
        couple = lax.dynamic_index_in_dim(upper_couple[step], side, 0, keepdims=False)
        term = jnp.dot(siblings[step], couple, preferred_element_type=jnp.float32)
        if local is not None:
            transfer = lax.dynamic_index_in_dim(upper_transfer[step], side, 0, keepdims=False)
            term = term + jnp.einsum(
                "rl,kl->rk", local, transfer, preferred_element_type=jnp.float32
            )
        local = term.astype(jnp.bfloat16)
    local = local[None]
    for step in range(local_levels):
        expanded = jnp.einsum(
            "jrl,skl->jsrk", local, local_transfer, preferred_element_type=jnp.float32
        )
        expanded = expanded.reshape(-1, columns, rank)
        if step < local_levels - 1:
            local = expanded.astype(jnp.bfloat16)
    first_leaf = device * leaf_dev - HW
    rim_coeff = extended(leaf_coeff, (("leaf", 0),), HW)
    far_index = far_list - first_leaf
    live = jnp.arange(far_list.shape[1], dtype=jnp.int32)[None, :] < far_count[:, None]
    picked = jnp.where(live[:, :, None, None], rim_coeff[far_index], jnp.zeros((), jnp.bfloat16))
    far = (
        jnp.einsum("gsrk,gskl->grl", picked, leaf_couple, preferred_element_type=jnp.float32)
        + expanded
    )
    leaf_local = far.astype(jnp.bfloat16)
    far_out = jnp.einsum("gkp,grk->rgp", full_basis, leaf_local, preferred_element_type=jnp.float32)
    rim_values = extended(values, (("leaf", 1),), HW * leaf_size)
    rim_points = extended(points, (("leaf", 1),), HW * leaf_size)
    rim_points = rim_points.reshape(3, leaf_dev + 2 * HW, leaf_size)
    own_points = points.reshape(3, leaf_dev, leaf_size)
    near_index = near_list - first_leaf
    rim_values = rim_values.reshape(columns, leaf_dev + 2 * HW, leaf_size)
    near = near_field(own_points, near_index, rim_points, rim_values, leaf_dev)
    return (near + far_out).reshape(columns, leaf_dev * leaf_size)


def solution(mesh):
    placed = (
        P("rhs", "leaf"),
        P(None, "leaf"),
        P("leaf", "rhs", None),
        P("leaf", None),
        P("leaf", None),
        P("leaf"),
        P("leaf", None, None, None),
        P(),
        P(),
        P(),
    )
    return jax.shard_map(
        on_device, mesh=mesh, in_specs=placed, out_specs=P("rhs", "leaf"), check_vma=False
    )
```

profile of v0, /device:TPU:32, one launch (start us, length us, event | category | flops | bytes accessed | tf_op | source)
XLA Modules:
  0.0 761.0 jit_solution(18369919923251736941)
XLA Ops:
  6.5 0.9 fusion.138
  7.4 3.8 collective-permute-start.1
  11.2 2.1 collective-permute-start
  13.3 0.7 fusion.142
  14.0 3.7 collective-permute-start.3
  17.8 2.1 collective-permute-start.2
  19.9 0.8 copy.28
  20.7 0.7 compare_select_fusion.1
  21.6 0.7 iota_compare_fusion
  22.3 1.0 fusion.140
  23.5 0.9 copy.75
  24.5 0.9 pad_maximum_fusion.2
  25.5 1.1 pad_maximum_fusion
  26.7 351.4 %while.10 = (s32[]{:T(128)}, f32[8,32,4,256]{3,1,2,0:T(8,128)}, s32[8]{0:T(128)S(1)}, s32[32,9]{1,0:T(8,128)S(1)}, bf16[32,40,256]{2,0,1:T(8,128)(2,1)S(1)}, /*i...) while((s32[]{:T(128)}, f32[8,32,4,256]{3,1,2,0:T(8,128)}, ...), condition=%wide.region_1.2_spmd, body=%wide.region_0.1_spmd.sunk | while | flops 181666928 | bytes 12375239 | solution.py:58
  26.7 0.7 dynamic_slice.184
  29.4 0.6 gather_fusion
  30.0 0.6 gather_fusion.1
  30.9 37.6 %multiply_convert_fusion.10 = bf16[4,9,256,256]{3,2,1,0:T(8,128)(2,1)S(1)} fusion(f32[4,9,256]{2,1,0:T(8,128)S(1)} %copy.82, f32[4,256]{1,0:T(4,128)S(1)} %get-tuple-element.152, f32[4,9,256]{2,1,0:T(8,128)S(1)} %copy.83, f32[4,256]{1,0:T(4,128)S(1)} %get-tuple-element.154, f32[4,9,256]{2,1,0:T(8,128)S(1)} %copy.85, ...), kind=kLoop, calls=%fused_computation.3.clone.clone.clone.clone.clone.clone.1.clone.1 | loop fusion | flops 30670848 | bytes 4841472 | tf_op jit(solution)/shard_map/while/body/eval_jaxpr/gnpq,rgnq->rgp/dot_general | solution.py:53
  68.5 2.1 fusion.173
  70.6 0.6 dynamic_slice.184
  73.3 0.6 gather_fusion
  73.9 0.6 gather_fusion.1
  74.8 37.6 %multiply_convert_fusion.10 = bf16[4,9,256,256]{3,2,1,0:T(8,128)(2,1)S(1)} fusion(f32[4,9,256]{2,1,0:T(8,128)S(1)} %copy.82, f32[4,256]{1,0:T(4,128)S(1)} %get-tuple-element.152, f32[4,9,256]{2,1,0:T(8,128)S(1)} %copy.83, f32[4,256]{1,0:T(4,128)S(1)} %get-tuple-element.154, f32[4,9,256]{2,1,0:T(8,128)S(1)} %copy.85, ...), kind=kLoop, calls=%fused_computation.3.clone.clone.clone.clone.clone.clone.1.clone.1 | loop fusion | flops 30670848 | bytes 4841472 | tf_op jit(solution)/shard_map/while/body/eval_jaxpr/gnpq,rgnq->rgp/dot_general | solution.py:53
  112.4 2.1 fusion.173
  114.6 0.6 dynamic_slice.184
  117.2 0.6 gather_fusion
  117.8 0.6 gather_fusion.1
  118.7 37.6 %multiply_convert_fusion.10 = bf16[4,9,256,256]{3,2,1,0:T(8,128)(2,1)S(1)} fusion(f32[4,9,256]{2,1,0:T(8,128)S(1)} %copy.82, f32[4,256]{1,0:T(4,128)S(1)} %get-tuple-element.152, f32[4,9,256]{2,1,0:T(8,128)S(1)} %copy.83, f32[4,256]{1,0:T(4,128)S(1)} %get-tuple-element.154, f32[4,9,256]{2,1,0:T(8,128)S(1)} %copy.85, ...), kind=kLoop, calls=%fused_computation.3.clone.clone.clone.clone.clone.clone.1.clone.1 | loop fusion | flops 30670848 | bytes 4841472 | tf_op jit(solution)/shard_map/while/body/eval_jaxpr/gnpq,rgnq->rgp/dot_general | solution.py:53
  156.4 2.1 fusion.173
  158.5 0.6 dynamic_slice.184
  161.2 0.6 gather_fusion
  161.8 0.6 gather_fusion.1
  162.6 37.6 %multiply_convert_fusion.10 = bf16[4,9,256,256]{3,2,1,0:T(8,128)(2,1)S(1)} fusion(f32[4,9,256]{2,1,0:T(8,128)S(1)} %copy.82, f32[4,256]{1,0:T(4,128)S(1)} %get-tuple-element.152, f32[4,9,256]{2,1,0:T(8,128)S(1)} %copy.83, f32[4,256]{1,0:T(4,128)S(1)} %get-tuple-element.154, f32[4,9,256]{2,1,0:T(8,128)S(1)} %copy.85, ...), kind=kLoop, calls=%fused_computation.3.clone.clone.clone.clone.clone.clone.1.clone.1 | loop fusion | flops 30670848 | bytes 4841472 | tf_op jit(solution)/shard_map/while/body/eval_jaxpr/gnpq,rgnq->rgp/dot_general | solution.py:53
  200.3 2.1 fusion.173
  202.4 0.6 dynamic_slice.184
  205.1 0.6 gather_fusion
  205.7 0.6 gather_fusion.1
  206.6 37.6 %multiply_convert_fusion.10 = bf16[4,9,256,256]{3,2,1,0:T(8,128)(2,1)S(1)} fusion(f32[4,9,256]{2,1,0:T(8,128)S(1)} %copy.82, f32[4,256]{1,0:T(4,128)S(1)} %get-tuple-element.152, f32[4,9,256]{2,1,0:T(8,128)S(1)} %copy.83, f32[4,256]{1,0:T(4,128)S(1)} %get-tuple-element.154, f32[4,9,256]{2,1,0:T(8,128)S(1)} %copy.85, ...), kind=kLoop, calls=%fused_computation.3.clone.clone.clone.clone.clone.clone.1.clone.1 | loop fusion | flops 30670848 | bytes 4841472 | tf_op jit(solution)/shard_map/while/body/eval_jaxpr/gnpq,rgnq->rgp/dot_general | solution.py:53
  244.2 2.1 fusion.173
  246.3 0.6 dynamic_slice.184
  249.0 0.6 gather_fusion
  249.6 0.6 gather_fusion.1
  250.5 37.6 %multiply_convert_fusion.10 = bf16[4,9,256,256]{3,2,1,0:T(8,128)(2,1)S(1)} fusion(f32[4,9,256]{2,1,0:T(8,128)S(1)} %copy.82, f32[4,256]{1,0:T(4,128)S(1)} %get-tuple-element.152, f32[4,9,256]{2,1,0:T(8,128)S(1)} %copy.83, f32[4,256]{1,0:T(4,128)S(1)} %get-tuple-element.154, f32[4,9,256]{2,1,0:T(8,128)S(1)} %copy.85, ...), kind=kLoop, calls=%fused_computation.3.clone.clone.clone.clone.clone.clone.1.clone.1 | loop fusion | flops 30670848 | bytes 4841472 | tf_op jit(solution)/shard_map/while/body/eval_jaxpr/gnpq,rgnq->rgp/dot_general | solution.py:53
  288.1 2.1 fusion.173
  290.3 0.6 dynamic_slice.184
  293.5 0.6 gather_fusion.1
  294.4 37.6 %multiply_convert_fusion.10 = bf16[4,9,256,256]{3,2,1,0:T(8,128)(2,1)S(1)} fusion(f32[4,9,256]{2,1,0:T(8,128)S(1)} %copy.82, f32[4,256]{1,0:T(4,128)S(1)} %get-tuple-element.152, f32[4,9,256]{2,1,0:T(8,128)S(1)} %copy.83, f32[4,256]{1,0:T(4,128)S(1)} %get-tuple-element.154, f32[4,9,256]{2,1,0:T(8,128)S(1)} %copy.85, ...), kind=kLoop, calls=%fused_computation.3.clone.clone.clone.clone.clone.clone.1.clone.1 | loop fusion | flops 30670848 | bytes 4841472 | tf_op jit(solution)/shard_map/while/body/eval_jaxpr/gnpq,rgnq->rgp/dot_general | solution.py:53
  332.1 2.1 fusion.173
  334.2 0.6 dynamic_slice.184
  336.9 0.6 gather_fusion
  337.5 0.6 gather_fusion.1
  338.3 37.6 %multiply_convert_fusion.10 = bf16[4,9,256,256]{3,2,1,0:T(8,128)(2,1)S(1)} fusion(f32[4,9,256]{2,1,0:T(8,128)S(1)} %copy.82, f32[4,256]{1,0:T(4,128)S(1)} %get-tuple-element.152, f32[4,9,256]{2,1,0:T(8,128)S(1)} %copy.83, f32[4,256]{1,0:T(4,128)S(1)} %get-tuple-element.154, f32[4,9,256]{2,1,0:T(8,128)S(1)} %copy.85, ...), kind=kLoop, calls=%fused_computation.3.clone.clone.clone.clone.clone.clone.1.clone.1 | loop fusion | flops 30670848 | bytes 4841472 | tf_op jit(solution)/shard_map/while/body/eval_jaxpr/gnpq,rgnq->rgp/dot_general | solution.py:53
  376.0 2.1 fusion.173
  378.1 1.6 convolution_convert_fusion
  380.8 347.6 %all-gather = bf16[4096,64]{1,0:T(8,128)(2,1)S(1)} all-gather(bf16[32,64]{1,0:T(8,128)(2,1)S(1)} %fusion.38), channel_id=2, replica_groups=mesh['leaf'=128,'rhs'=2] {'leaf'}, dimensions={0}, use_global_device_ids=true | all-gather | bytes 528384 | tf_op jit(solution)/shard_map/all_gather | solution.py:92
  728.4 1.1 fusion.11
  729.5 0.7 fusion.21
  733.4 6.6 collective-permute-start.5
  740.0 1.9 collective-permute-start.4
  741.9 1.1 fusion.53
  743.0 2.8 collective-permute-done.4
  745.9 1.0 gather_fusion.2
  746.9 4.9 fusion.10
  751.8 2.3 copy.54
  (128 shorter events, 7.4 us)
Async XLA Ops:
  6.5 373.2 %copy-start = (bf16[2,64,64]{2,1,0:T(8,128)(2,1)S(1)}, bf16[2,64,64]{2,1,0:T(8,128)(2,1)}, u32[]{:S(2)}) copy-start(bf16[2,64,64]{2,1,0:T(8,128)(2,1)} %param.19) | copy-start | bytes 49156
  6.5 371.6 %all-gather.3.cloned.1.call-start = ((), (), s32[]{:S(2)}) async-start(), calls=%async_computation | async-start | bytes 1572864 | tf_op jit(solution)/shard_map/all_gather | solution.py:81
  7.4 18.1 %collective-permute-start.1 = (bf16[32,1024]{1,0:T(8,128)(2,1)S(1)}, bf16[32,1024]{1,0:T(8,128)(2,1)S(1)}, u32[]{:S(2)}, u32[]{:S(2)}) collective-permute-start(bf16[32,1024]{1,0:T(8,128)(2,1)S(1)} %get-tuple-element.73), channel_id=1, source_target_pairs={{2,0},{4,2},{6,4},{8,6},{10,8},{12,10},{14,12},{16,14},{18,16},{20... | collective-permute-start | bytes 196616 | tf_op jit(solution)/shard_map/ppermute | solution.py:23
  11.2 14.3 %collective-permute-start = (bf16[32,1024]{1,0:T(8,128)(2,1)S(1)}, bf16[32,1024]{1,0:T(8,128)(2,1)S(1)}, u32[]{:S(2)}, u32[]{:S(2)}) collective-permute-start(bf16[32,1024]{1,0:T(8,128)(2,1)S(1)} %get-tuple-element.72), channel_id=1, source_target_pairs={{0,2},{2,4},{4,6},{6,8},{8,10},{10,12},{12,14},{14,16},{16,18},{18... | collective-permute-start | bytes 196616 | tf_op jit(solution)/shard_map/ppermute | solution.py:20
  14.0 10.5 %collective-permute-start.3 = (f32[3,1024]{1,0:T(4,128)S(1)}, f32[3,1024]{1,0:T(4,128)S(1)}, u32[]{:S(2)}, u32[]{:S(2)}) collective-permute-start(f32[3,1024]{1,0:T(4,128)S(1)} %get-tuple-element.90), channel_id=1, source_target_pairs={{2,0},{4,2},{6,4},{8,6},{10,8},{12,10},{14,12},{16,14},{18,16},{20... | collective-permute-start | bytes 36872 | tf_op jit(solution)/shard_map/ppermute | solution.py:23
  17.8 6.8 collective-permute-start.2
  26.7 351.4 %copy-start.2 = (bf16[32,8192]{1,0:T(8,128)(2,1)S(1)}, bf16[32,8192]{1,0:T(8,128)(2,1)}, u32[]{:S(2)}) copy-start(bf16[32,8192]{1,0:T(8,128)(2,1)} %param.12) | copy-start | bytes 1572868
  26.7 701.7 %copy-start.3 = (bf16[7,2,64,64]{3,2,1,0:T(8,128)(2,1)S(1)}, bf16[7,2,64,64]{3,2,1,0:T(8,128)(2,1)}, u32[]{:S(2)}) copy-start(bf16[7,2,64,64]{3,2,1,0:T(8,128)(2,1)} %param.20) | copy-start | bytes 344068
  728.4 18.5 %copy-start.1 = (bf16[32,64,256]{2,1,0:T(8,128)(2,1)S(1)}, bf16[32,64,256]{2,1,0:T(8,128)(2,1)}, u32[]{:S(2)}) copy-start(bf16[32,64,256]{2,1,0:T(8,128)(2,1)} %all-gather.3.cloned.1.call-done) | copy-start | bytes 3145732
  733.4 9.6 %collective-permute-start.5 = (bf16[4,32,64]{2,1,0:T(8,128)(2,1)S(1)}, bf16[4,32,64]{2,1,0:T(8,128)(2,1)S(1)}, u32[]{:S(2)}, u32[]{:S(2)}) collective-permute-start(bf16[4,32,64]{2,1,0:T(8,128)(2,1)S(1)} %get-tuple-element.75), channel_id=1, source_target_pairs={{2,0},{4,2},{6,4},{8,6},{10,8},{12,10},{14,12},{16,14},{18,16},{20... | collective-permute-start | bytes 49160 | tf_op jit(solution)/shard_map/ppermute | solution.py:23
  740.0 5.8 collective-permute-start.4
Sparse Core Ops, SparseCore 0:
  20.0 23.8 all-gather.2
where the time goes:
time: 762 us; the launch traced here: 761 us
  blocking collectives  348 us (46%)
  other arithmetic  305 us (40%)
  matrix products  30.7 us (4%)
  local copies, waits for them, and re-layouts  25 us (3%)
  starting transfers between devices  20.2 us (3%)
  loops' own time  15.9 us (2%)
  between operations  13.9 us (2%)
    all_gather x1, blocking collectives, on_device(): nodes = lax.all_gather(level, 'leaf', axis=0, tiled=True)  348 us
    dot_general x8, other arithmetic, near_block(): jnp.einsum('gnpq,rgnq->rgp', kernel, rim_values[:, index], preferred_elem...  301 us
    dot_general x8, matrix products, near_block(): jnp.einsum('gnpq,rgnq->rgp', kernel, rim_values[:, index], preferred_elem...  17.1 us
    another operation x1, loops' own time, near_field(): blocks = lax.map(near_block, starts)  15.9 us
  transfers between devices with their start and end apart: 7, of which 1 were waited for; matrix products, arithmetic and copies ran while one was open for 45% of the time, Pallas kernels for 0%

commit v1 on v0

v1 whole, which is shorter than its diff:
```python
import functools
import math

import jax
import jax.numpy as jnp
import numpy as np
from jax import lax
from jax.experimental import pallas as pl
from jax.experimental.pallas import tpu as pltpu
from jax.sharding import PartitionSpec as P

MESH = pl.DeviceIdType.MESH
F32 = jnp.float32
BF16 = jnp.bfloat16
HW = 4
WAVE = 20.0
SMOOTH = 0.05
LEAF = 256
OWN = 16
EXT = OWN + 2 * HW
SCALE = WAVE / (2 * math.pi)
SOFT = SCALE * SCALE * SMOOTH * SMOOTH
DEGREE = 5


def cosine_fit():
    nodes = 0.125 + 0.125 * np.cos(np.pi * (np.arange(64) + 0.5) / 64)
    series = np.polynomial.chebyshev.Chebyshev.fit(
        nodes, np.cos(2 * np.pi * np.sqrt(nodes)), DEGREE, domain=[0, 0.25]
    )
    power = series.convert(kind=np.polynomial.Polynomial).coef
    return [float(v) for v in power * SCALE / math.sqrt(9 * LEAF)]


COSINE = cosine_fit()


def entries(scaled):
    scaled = jnp.maximum(scaled, 1e-12)
    turns = scaled * lax.rsqrt(scaled)
    rest = turns - jnp.round(turns)
    square = rest * rest
    poly = COSINE[DEGREE]
    for power in range(DEGREE - 1, -1, -1):
        poly = poly * square + COSINE[power]
    return (poly * lax.rsqrt(scaled + SOFT)).astype(BF16)


def dot(a, b, left=1, right=0):
    return lax.dot_general(a, b, (((left,), (right,)), ((), ())), preferred_element_type=F32)


def cols(leaf, count=1):
    return pl.ds(pl.multiple_of(leaf * LEAF, LEAF), count * LEAF)


def diagonal(block):
    block = block.astype(F32)
    zero = jnp.zeros_like(block)
    top = jnp.concatenate([block, zero], axis=1)
    low = jnp.concatenate([zero, block], axis=1)
    return jnp.concatenate([top, low], axis=0).astype(BF16)


def kernel(
    n,
    zn,
    values,
    points,
    basis,
    near_list,
    far_list,
    far_count,
    couple,
    local_transfer,
    upper_transfer,
    upper_couple,
    out,
    vx,
    px,
    fa,
    fb,
    bx,
    cv,
    acc,
    dco,
    lev,
    ldown,
    nodes,
    pair,
    zb,
    gb,
    wup,
    wdn,
    wld,
    wleaf,
    count,
    loc,
    ssem,
    rsem,
    zs,
    zr,
    gs,
    gr,
    osem,
):
    d = lax.axis_index("leaf")
    c = lax.axis_index("rhs")
    p = 1 - c
    gn = n // zn
    z = lax.rem(d, zn)
    g = d // zn
    after = lax.rem(d + 1, n)
    before = lax.rem(d + n - 1, n)
    upl = (n - 1).bit_length()
    zl = (zn - 1).bit_length()

    barrier = pltpu.get_barrier_semaphore()

    def greet(leaf, core):
        pl.semaphore_signal(barrier, inc=1, device_id=(leaf, core), device_id_type=MESH)

    side_dev = lax.rem(d + n - 1 + 2 * c, n)
    greet(d, p)
    greet(side_dev, 0)
    greet(side_dev, 1)

    @pl.loop(1, zn)
    def _(t):
        greet(g * zn + lax.rem(z + t, zn), c)

    @pl.loop(1, gn)
    def _(t):
        greet(lax.rem(g + t, gn) * zn + z, c)

    def local(src, dst, k):
        copy = pltpu.make_async_copy(src, dst, loc.at[k])
        copy.start()
        return copy

    lp = local(points.at[:, cols(12 * c, 20)], px.at[:, cols(4 - 4 * c, 20)], 0)
    lv = local(
        values.at[:, cols(12 * c, 20)], vx.at[pl.ds(32 * c, 32), cols(4 - 4 * c, 20)], 1
    )
    lb = local(basis.at[pl.ds(16 * c, 16)], bx.at[:, pl.ds(32 * c, 32), :], 2)
    lc = local(couple.at[pl.ds(16 * c, 16)], cv, 3)

    pl.semaphore_wait(barrier, 3 + (zn - 1) + (gn - 1))

    def send(src, dst, k, r, leaf, core):
        copy = pltpu.make_async_remote_copy(
            src_ref=src,
            dst_ref=dst,
            send_sem=ssem.at[k],
            recv_sem=rsem.at[r],
            device_id=(leaf, core),
            device_id_type=MESH,
        )
        copy.start()
        return copy

    own = pl.ds(32 * c, 32)
    sv = send(values.at[:, cols(12 * p, 20)], vx.at[own, cols(4 - 4 * p, 20)], 0, 0, d, p)
    sb = send(basis.at[pl.ds(16 * p, 16)], bx.at[:, own, :], 1, 1, d, p)
    sp = send(
        points.at[:, cols(28 * p, 4)],
        px.at[:, cols(20 * c, 4)],
        2,
        2,
        lax.rem(d + n + 1 - 2 * c, n),
        c,
    )
    sr0 = send(values.at[:, cols(28, 4)], vx.at[own, cols(0, 4)], 3, 3 + c, after, 0)
    sr1 = send(values.at[:, cols(0, 4)], vx.at[own, cols(20, 4)], 4, 3 + c, before, 1)

    for s in range(2):
        t = local_transfer[s]
        wup[0, pl.ds(128 * s, 128), :] = diagonal(t)
        td = t.astype(F32).T
        wld[s] = diagonal(td)
        zero = jnp.zeros((64, 64), F32)
        wide = jnp.concatenate([td, zero], axis=1).astype(BF16)
        none = jnp.zeros((64, 128), BF16)
        wleaf[0, pl.ds(0, 64), pl.ds(128 * s, 128)] = wide
        wleaf[0, pl.ds(64, 64), pl.ds(128 * s, 128)] = none
        wleaf[1, pl.ds(0, 64), pl.ds(128 * s, 128)] = none
        wleaf[1, pl.ds(64, 64), pl.ds(128 * s, 128)] = wide

    @pl.loop(0, upl)
    def _(u):
        for s in range(2):
            t = upper_transfer[u, s]
            wup[u + 1, pl.ds(128 * s, 128), :] = diagonal(t)
            wdn[2 * u + s, pl.ds(0, 128), :] = diagonal(upper_couple[u, s])
            wdn[2 * u + s, pl.ds(128, 128), :] = diagonal(t.astype(F32).T)

    @pl.loop(0, OWN)
    def _(i):
        row = 16 * c + i
        slots = [near_list[s, row] - (d * 32 + row) for s in range(9)]
        for o in range(9):
            total = jnp.float32(0)
            for s in range(9):
                total = total + jnp.where(slots[s] == o - HW, jnp.float32(1), jnp.float32(0))
            count[i * 9 + o] = total

    @pl.loop(0, HW * 9)
    def _(i):
        count[OWN * 9 + i] = jnp.float32(0)

    acc[...] = jnp.zeros_like(acc)
    dco[EXT] = jnp.zeros((64, 128), BF16)

    rows = lax.broadcasted_iota(jnp.int32, (8, LEAF), 0)

    def factors(e):
        at = cols(e)
        x = (px[:, at] - 0.5) * SCALE
        x = jnp.concatenate([x, jnp.zeros((5, LEAF), F32)], axis=0)
        high = x.astype(BF16).astype(F32)
        low = (x - high).astype(BF16).astype(F32)
        both = high + low
        norm = jnp.sum(both * both, axis=0, keepdims=True)
        n1 = norm.astype(BF16).astype(F32)
        n2 = (norm - n1).astype(BF16).astype(F32)
        n3 = (norm - n1 - n2).astype(BF16).astype(F32)
        norms = jnp.where(
            rows == 3, n1, jnp.where(rows == 4, n2, jnp.where(rows == 5, n3, 0.0))
        )
        ones = jnp.where((rows >= 3) & (rows <= 5), 1.0, 0.0)
        fa[:, at] = jnp.concatenate([high + norms, high + ones, low, low], axis=0).astype(BF16)
        fb[:, at] = jnp.concatenate(
            [ones - 2 * high, norms - 2 * low, -2 * high, -2 * low], axis=0
        ).astype(BF16)

    lp.wait()

    @pl.loop(0, 20)
    def _(e):
        factors(e + 4 - 4 * c)

    def near_main(i):
        e = i + HW
        left = fa[:, cols(e)]
        mine = vx[:, cols(e)]
        total = None
        parts = []
        for o in range(HW + 1):
            block = entries(dot(left, fb[:, cols(e + o)], 0, 0))
            term = dot(vx[:, cols(e + o)], block, 1, 1) * count[i * 9 + HW + o]
            total = term if total is None else total + term
            if o:
                parts.append(dot(mine, block, 1, 0) * count[(i + o) * 9 + HW - o])
        acc[:, cols(e, HW + 1)] += jnp.concatenate([total] + parts, axis=1)

    def near_rim(w):
        for b in range(HW + 1):
            first = b < HW - w
            e = jnp.where(first, w + b, b - 1)
            j = jnp.where(first, w, 3 - w)
            block = entries(dot(fa[:, cols(e)], fb[:, cols(j + HW)], 0, 0))
            acc[:, cols(j + HW)] += dot(vx[:, cols(e)], block, 1, 0) * count[j * 9 + e - j]

    def batch(start):
        @pl.loop(start, start + 4, step=2)
        def _(i):
            near_main(i)
            near_main(i + 1)

    lv.wait()
    sv.wait_recv()
    lb.wait()
    sb.wait_recv()
    lanes = lax.broadcasted_iota(jnp.int32, (32, 128), 1) < 64

    @pl.loop(0, OWN, step=4)
    def _(i0):
        for k in range(4):
            i = i0 + k
            twice = jnp.concatenate([bx[i], bx[i]], axis=0)
            full = dot(vx[:, cols(i + HW)], twice, 1, 1)
            dco[i + HW] = full.astype(BF16)
            lev[i] = jnp.where(lanes, full[0:32], full[32:64]).astype(BF16)

    sc0 = send(
        dco.at[pl.ds(4, 4)], dco.at[pl.ds(20, 4)], 5, 5, lax.rem(d + n - p, n), p
    )
    sc1 = send(dco.at[pl.ds(16, 4)], dco.at[pl.ds(0, 4)], 6, 6, lax.rem(d + c, n), p)

    def joined(read, m):
        return jnp.concatenate(
            [
                jnp.concatenate([read(2 * j), read(2 * j + 1)], axis=1)
                for j in range(m)
            ],
            axis=0,
        )

    def upward(src, at, dst, to, m, weight):
        whole = dot(joined(lambda j: src[at + j], m), wup[weight]).astype(BF16)
        for j in range(m):
            dst[to + j] = whole[32 * j : 32 * j + 32]

    upward(lev, 0, lev, 16, 8, 0)
    upward(lev, 16, lev, 24, 4, 0)
    upward(lev, 24, lev, 28, 2, 0)
    whole = dot(joined(lambda j: lev[28 + j], 1), wup[0]).astype(BF16)
    lev[30] = whole
    pair[c] = whole
    sn = send(lev.at[30], pair.at[c], 7, 7, d, p)

    batch(0)

    sn.wait_recv()
    root = dot(joined(lambda j: pair[j], 1), wup[0]).astype(BF16)
    zb[z] = root

    def ring(buf, slot, sems, recvs, t, leaf):
        return pltpu.make_async_remote_copy(
            src_ref=buf.at[slot],
            dst_ref=buf.at[slot],
            send_sem=sems.at[t],
            recv_sem=recvs.at[t],
            device_id=(leaf, c),
            device_id_type=MESH,
        )

    def z_copy(t):
        return ring(zb, z, zs, zr, t - 1, g * zn + lax.rem(z + t, zn))

    def g_copy(t):
        return ring(gb, g, gs, gr, t - 1, lax.rem(g + t, gn) * zn + z)

    @pl.loop(1, zn)
    def _(t):
        z_copy(t).start()

    batch(4)

    @pl.loop(1, zn)
    def _(t):
        z_copy(t).wait_recv()

    at = 0
    m = zn
    weight = 1
    while m > 2:
        upward(zb, at, zb, at + m, m // 2, weight)
        at, m, weight = at + m, m // 2, weight + 1
    gb[g] = dot(joined(lambda j: zb[at + j], 1), wup[weight]).astype(BF16)
    weight += 1

    @pl.loop(1, gn)
    def _(t):
        g_copy(t).start()

    batch(8)

    sp.wait_recv()

    @pl.loop(0, 4)
    def _(e):
        factors(e + 20 * c)

    for r in range(2):
        pltpu.make_async_copy(
            vx.at[pl.ds(0, 32), cols(0, 4)], vx.at[pl.ds(0, 32), cols(0, 4)], rsem.at[3 + r]
        ).wait()

    batch(12)

    @pl.loop(0, 2)
    def _(w):
        near_rim(w)

    @pl.loop(1, gn)
    def _(t):
        g_copy(t).wait_recv()

    at = 0
    m = gn
    while m > 2:
        upward(gb, at, gb, at + m, m // 2, weight)
        at, m, weight = at + m, m // 2, weight + 1

    down = jnp.zeros((32, 128), BF16)
    for u in range(upl - 1, -1, -1):
        if u >= zl:
            buf, size, index, step = gb, gn, g, u - zl
        else:
            buf, size, index, step = zb, zn, z, u
        base = 2 * size - 2 * (size >> step)
        here = index // 2**step
        side = lax.rem(here, 2)
        sibling = buf[base + here + 1 - 2 * side]
        both = jnp.concatenate([sibling, down], axis=1)
        down = dot(both, wdn[2 * u + side]).astype(BF16)
    nodes[0] = dot(down, wld[c]).astype(BF16)
    at, m = 0, 1
    while m < 8:
        whole = jnp.concatenate([nodes[at + j] for j in range(m)], axis=0)
        for s in range(2):
            child = dot(whole, wld[s]).astype(BF16)
            for j in range(m):
                nodes[at + m + 2 * j + s] = child[32 * j : 32 * j + 32]
        at, m = at + m, 2 * m
    whole = jnp.concatenate([nodes[at + j] for j in range(8)], axis=0)
    for h in range(2):
        low = dot(whole, wleaf[h])
        for j in range(8):
            for s in range(2):
                ldown[2 * j + s, pl.ds(32 * h, 32), :] = low[
                    32 * j : 32 * j + 32, 128 * s : 128 * s + 128
                ]

    sc0.wait_recv()
    sc1.wait_recv()
    lc.wait()
    wide = lax.broadcasted_iota(jnp.int32, (64, 128), 1) < 64
    pick0 = jnp.where(wide, 1.0, 0.0).astype(BF16)
    pick1 = jnp.where(wide, 0.0, 1.0).astype(BF16)

    def result(i):
        row = 16 * c + i
        first = d * 32 + 16 * c - HW
        used = far_count[row]
        at = [jnp.where(s < used, far_list[s, row] - first, EXT) for s in range(8)]
        coeffs = jnp.concatenate(
            [dco[at[2 * q]] * pick0 + dco[at[2 * q + 1]] * pick1 for q in range(4)], axis=1
        )
        far = dot(coeffs, cv[i].reshape(512, 64)) + ldown[i][:, 0:64]
        acc[:, cols(i + HW)] += dot(far.astype(BF16), bx[i])

    def out_local(k):
        return pltpu.make_async_copy(
            acc.at[own, cols(HW + 4 * k, 4)], out.at[:, cols(16 * c + 4 * k, 4)], loc.at[4 + k]
        )

    def out_send(k):
        return pltpu.make_async_remote_copy(
            src_ref=acc.at[pl.ds(32 * p, 32), cols(HW + 4 * k, 4)],
            dst_ref=out.at[:, cols(16 * c + 4 * k, 4)],
            send_sem=osem.at[k],
            recv_sem=osem.at[4 + k],
            device_id=(d, p),
            device_id_type=MESH,
        )

    @pl.loop(0, 4)
    def _(k):
        for i in range(4):
            result(4 * k + i)
        out_send(k).start()
        out_local(k).start()

    for copy in (sv, sb, sp, sr0, sr1, sc0, sc1, sn):
        copy.wait_send()

    @pl.loop(1, zn)
    def _(t):
        z_copy(t).wait_send()

    @pl.loop(1, gn)
    def _(t):
        g_copy(t).wait_send()

    @pl.loop(0, 4)
    def _(k):
        out_local(k).wait()
        out_send(k).wait()


def solution(mesh):
    n = mesh.shape["leaf"]
    zn = 8 if n >= 64 else 2
    gn = n // zn
    upl = (n - 1).bit_length()
    hbm = pl.BlockSpec(memory_space=pl.ANY)
    vmem = pl.BlockSpec(memory_space=pltpu.VMEM)
    smem = pl.BlockSpec(memory_space=pltpu.SMEM)
    dma = pltpu.SemaphoreType.DMA

    def on_device(values, points, basis, near_list, far_list, *rest):
        return pl.pallas_call(
            functools.partial(kernel, n, zn),
            out_shape=jax.ShapeDtypeStruct((32, 8192), F32),
            in_specs=[hbm, hbm, hbm, smem, smem, smem, hbm, vmem, vmem, vmem],
            out_specs=hbm,
            scratch_shapes=[
                pltpu.VMEM((64, EXT * LEAF), BF16),
                pltpu.VMEM((3, EXT * LEAF), F32),
                pltpu.VMEM((32, EXT * LEAF), BF16),
                pltpu.VMEM((32, EXT * LEAF), BF16),
                pltpu.VMEM((OWN, 64, LEAF), BF16),
                pltpu.VMEM((OWN, 8, 64, 64), BF16),
                pltpu.VMEM((64, EXT * LEAF), F32),
                pltpu.VMEM((EXT + 1, 64, 128), BF16),
                pltpu.VMEM((32, 32, 128), BF16),
                pltpu.VMEM((OWN, 64, 128), F32),
                pltpu.VMEM((16, 32, 128), BF16),
                pltpu.VMEM((2, 32, 128), BF16),
                pltpu.VMEM((2 * zn, 32, 128), BF16),
                pltpu.VMEM((2 * gn, 32, 128), BF16),
                pltpu.VMEM((upl + 1, 256, 128), BF16),
                pltpu.VMEM((2 * upl, 256, 128), BF16),
                pltpu.VMEM((2, 128, 128), BF16),
                pltpu.VMEM((2, 128, 256), BF16),
                pltpu.SMEM(((OWN + HW) * 9,), F32),
                dma((8,)),
                dma((8,)),
                dma((8,)),
                dma((zn - 1,)),
                dma((zn - 1,)),
                dma((gn - 1,)),
                dma((gn - 1,)),
                dma((8,)),
            ],
            compiler_params=pltpu.CompilerParams(
                collective_id=0, has_side_effects=True, vmem_limit_bytes=60 * 2**20
            ),
            name="h2_matvec",
        )(values, points, basis, near_list.T, far_list.T, *rest)

    placed = (
        P("rhs", "leaf"),
        P(None, "leaf"),
        P("leaf", "rhs", None),
        P("leaf", None),
        P("leaf", None),
        P("leaf"),
        P("leaf", None, None, None),
        P(),
        P(),
        P(),
    )
    return jax.shard_map(
        on_device, mesh=mesh, in_specs=placed, out_specs=P("rhs", "leaf"), check_vma=False
    )
```

time: 762 us -> 55.6 us (0.07)
  the two profiles are of different devices: /device:TPU:32 before, /device:TPU:1 now
where the time goes in v1:
time: 55.6 us; the launch traced here: 55.5 us
  Pallas kernels  53.2 us (96%)
  local copies, waits for them, and re-layouts  2.26 us (4%)
    pallas_call x1, Pallas kernels, on_device(): pl.pallas_call(functools.partial(kernel, n, zn), out_shape=jax.ShapeDtype...  53.2 us
    unnamed x1, local copies, waits for them, and re-layouts  2.26 us

profile of v1, /device:TPU:1, one launch (start us, length us, event | category | flops | bytes accessed | tf_op | source)
XLA Modules:
  0.0 55.5 jit_solution(4531698164534715913)
XLA Ops:
  0.0 53.2 %h2_matvec.1 = f32[32,8192]{1,0:T(8,128)} custom-call(bf16[32,8192]{1,0:T(8,128)(2,1)} %values.1, f32[3,8192]{1,0:T(4,128)} %points.1, bf16[32,32,256]{2,1,0:T(8,128)(2,1)} %basis.1, s32[9,32]{1,0:T(8,128)} %bitcast.2, s32[8,32]{1,0:T(8,128)} %bitcast.3, s32[32]{0:T(128)} %far_count.1, bf16[32,8,64,64]{3,2,1,0:T(8,128)(2,1)} %couple.1, ...), custom_call_target="tpu_custom_call" | custom-call | tf_op jit(solution)/shard_map/h2_matvec/pallas_call | solution.py:484
  53.2 2.3 %copy.12 = f32[32,8192]{1,0:T(8,128)} copy(f32[32,8192]{1,0:T(8,128)} %h2_matvec.1) | data formatting | bytes 2097152

commit v2 on v0

v2 whole, which is shorter than its diff:
```python
import functools
import math

import jax
import jax.numpy as jnp
import numpy as np
from jax import lax
from jax.experimental import pallas as pl
from jax.experimental.pallas import tpu as pltpu
from jax.sharding import PartitionSpec as P

MESH = pl.DeviceIdType.MESH
F32 = jnp.float32
BF16 = jnp.bfloat16
HW = 4
WAVE = 20.0
SMOOTH = 0.05
LEAF = 256
OWN = 16
EXT = OWN + 2 * HW
SCALE = WAVE / (2 * math.pi)
SOFT = SCALE * SCALE * SMOOTH * SMOOTH
DEGREE = 4
SCHEDULE = (
    (5, 5, 8, 10, 14, 5),
    (4, 5, 7, 10, 13, 4),
    (4, 4, 6, 9, 12, 4),
    (3, 3, 5, 8, 10, 3),
    (2, 2, 4, 7, 9, 2),
)


def cosine_fit():
    nodes = 0.125 + 0.125 * np.cos(np.pi * (np.arange(64) + 0.5) / 64)
    series = np.polynomial.chebyshev.Chebyshev.fit(
        nodes, np.cos(2 * np.pi * np.sqrt(nodes)), DEGREE, domain=[0, 0.25]
    )
    power = series.convert(kind=np.polynomial.Polynomial).coef
    return [float(v) for v in power * SCALE / math.sqrt(9 * LEAF)]


COSINE = cosine_fit()


def entries(scaled):
    scaled = jnp.maximum(scaled, 1e-12)
    turns = scaled * lax.rsqrt(scaled)
    rest = turns - jnp.round(turns)
    square = rest * rest
    poly = COSINE[DEGREE]
    for power in range(DEGREE - 1, -1, -1):
        poly = poly * square + COSINE[power]
    return (poly * lax.rsqrt(scaled + SOFT)).astype(BF16)


def dot(a, b, left=1, right=0):
    return lax.dot_general(a, b, (((left,), (right,)), ((), ())), preferred_element_type=F32)


def cols(leaf, count=1):
    return pl.ds(pl.multiple_of(leaf * LEAF, LEAF), count * LEAF)


def diagonal(block):
    block = block.astype(F32)
    zero = jnp.zeros_like(block)
    top = jnp.concatenate([block, zero], axis=1)
    low = jnp.concatenate([zero, block], axis=1)
    return jnp.concatenate([top, low], axis=0).astype(BF16)


def kernel(
    dims,
    values,
    points,
    basis,
    near_list,
    far_list,
    far_count,
    couple,
    local_transfer,
    upper_transfer,
    upper_couple,
    out,
    vx,
    px,
    fa,
    fb,
    bx,
    cv,
    kb,
    acc,
    dco,
    fco,
    lev,
    ldown,
    yfar,
    nodes,
    pair,
    zb,
    xb,
    yb,
    wup,
    wdn,
    wld,
    wsel,
    wleaf,
    tally,
    tally_next,
    count,
    count_next,
    spill,
    loc,
    ssem,
    rsem,
    zs,
    zr,
    xs,
    xr,
    ys,
    yr,
):
    yn, xn, zn = dims
    n = yn * xn * zn
    d = lax.axis_index("leaf")
    c = lax.axis_index("rhs")
    p = 1 - c
    z = lax.rem(d, zn)
    x = lax.rem(d // zn, xn)
    y = d // (zn * xn)
    after = lax.rem(d + 1, n)
    before = lax.rem(d + n - 1, n)
    beside = lax.rem(d + n - 1 + 2 * c, n)
    upl = (n - 1).bit_length()
    own = pl.ds(32 * c, 32)

    barrier = pltpu.get_barrier_semaphore()

    def greet(leaf, core):
        pl.semaphore_signal(barrier, inc=1, device_id=(leaf, core), device_id_type=MESH)

    def z_peer(t):
        return d - z + lax.rem(z + t, zn)

    def x_peer(t):
        return d + (lax.rem(x + t, xn) - x) * zn

    def y_peer(t):
        return d + (lax.rem(y + t, yn) - y) * zn * xn

    stages = (
        (zb, zn, z, zs, zr, z_peer),
        (xb, xn, x, xs, xr, x_peer),
        (yb, yn, y, ys, yr, y_peer),
    )

    greet(d, p)
    greet(before, 1)
    greet(after, 0)

    @pl.when(c == 1)
    def _():
        greet(after, 1)

    for _, size, _, _, _, peer in stages:

        @pl.loop(1, size)
        def _(t):
            greet(peer(t), c)

    def local(src, dst, k):
        return pltpu.make_async_copy(src, dst, loc.at[k])

    lp = local(points.at[:, cols(12 * c, 20)], px.at[:, cols(4 - 4 * c, 20)], 0)
    lv = local(
        values.at[:, cols(12 * c, 20)], vx.at[own, cols(4 - 4 * c, 20)], 1
    )
    lb = local(basis, bx.at[:, own, :], 2)
    lc = local(couple, cv, 3)
    lf = local(dco.at[:, own, :], fco.at[pl.ds(16 * c + HW, OWN)], 4)
    lt = local(tally, count, 6)
    lu = local(tally_next, count_next, 7)
    ln = local(acc.at[own, cols(HW, OWN)], out.at[:, cols(16 * c, OWN)], 5)
    for copy in (lp, lv, lb, lc):
        copy.start()

    def remote(src, dst, k, r, leaf, core):
        return pltpu.make_async_remote_copy(
            src_ref=src,
            dst_ref=dst,
            send_sem=ssem.at[k],
            recv_sem=rsem.at[r],
            device_id=(leaf, core),
            device_id_type=MESH,
        )

    sv = remote(values.at[:, cols(12 * p, 20)], vx.at[own, cols(4 - 4 * p, 20)], 0, 0, d, p)
    sb = remote(
        basis.at[pl.ds(16 * p, 16)], bx.at[pl.ds(16 * p, 16), own, :], 1, 1, d, p
    )
    sl = remote(
        basis.at[pl.ds(16 * c, 16)], bx.at[pl.ds(16 * c, 16), own, :], 2, 2, d, p
    )
    sp = remote(points.at[:, cols(0, 4)], px.at[:, cols(20, 4)], 3, 3, before, 1)
    st = remote(tally, tally_next, 4, 11, before, 1)
    sr = remote(values.at[:, cols(0, 4)], vx.at[own, cols(20, 4)], 5, 4 + c, before, 1)
    ss = remote(
        acc.at[:, cols(20, 4)], spill, 11, 12, lax.rem(d + c, n), p
    )
    sc = remote(
        dco.at[:, pl.ds(32 * p, 32), :], fco.at[pl.ds(16 * c + HW, OWN)], 6, 6, d, p
    )
    se0, se1 = [
        remote(
            dco.at[pl.ds(12 * c, HW), pl.ds(32 * q, 32), :],
            fco.at[pl.ds(36 * p, HW)],
            7 + q,
            7 + c,
            beside,
            q,
        )
        for q in range(2)
    ]
    sn = remote(lev.at[30], pair.at[c], 9, 9, d, p)
    so = remote(
        acc.at[pl.ds(32 * p, 32), cols(HW, OWN)], out.at[:, cols(16 * c, OWN)], 10, 10, d, p
    )

    def arrived(ref, r):
        pltpu.make_async_copy(ref, ref, rsem.at[r]).wait()

    def ring(stage, t):
        buf, size, me, sems, recvs, peer = stage
        return pltpu.make_async_remote_copy(
            src_ref=buf.at[me],
            dst_ref=buf.at[me],
            send_sem=sems.at[t - 1],
            recv_sem=recvs.at[t - 1],
            device_id=(peer(t), c),
            device_id_type=MESH,
        )

    def ring_start(stage):
        @pl.loop(1, stage[1])
        def _(t):
            ring(stage, t).start()

    def ring_recv(stage):
        @pl.loop(1, stage[1])
        def _(t):
            ring(stage, t).wait_recv()

    def weights():
        zero = jnp.zeros((64, 64), F32)
        none = jnp.zeros((64, 128), BF16)
        for s in range(2):
            t = local_transfer[s]
            wup[0, pl.ds(128 * s, 128), :] = diagonal(t)
            td = t.astype(F32).T
            wld[:, pl.ds(128 * s, 128)] = diagonal(td)
            wsel[pl.ds(64 * c, 64), pl.ds(128 * s, 128)] = jnp.concatenate(
                [td, td], axis=1
            ).astype(BF16)
            wsel[pl.ds(64 * p, 64), pl.ds(128 * s, 128)] = none
            wide = jnp.concatenate([td, zero], axis=1).astype(BF16)
            wleaf[0, pl.ds(0, 64), pl.ds(128 * s, 128)] = wide
            wleaf[0, pl.ds(64, 64), pl.ds(128 * s, 128)] = none
            wleaf[1, pl.ds(0, 64), pl.ds(128 * s, 128)] = none
            wleaf[1, pl.ds(64, 64), pl.ds(128 * s, 128)] = wide
        for u in range(upl):
            for s in range(2):
                t = upper_transfer[u, s]
                if u < upl - 1:
                    wup[u + 1, pl.ds(128 * s, 128), :] = diagonal(t)
                wdn[2 * u + s, pl.ds(0, 128), :] = diagonal(upper_couple[u, s])
                wdn[2 * u + s, pl.ds(128, 128), :] = diagonal(t.astype(F32).T)

    def counts():
        leaf = lax.broadcasted_iota(jnp.int32, (9, 32), 1)
        offset = near_list[...] - leaf - d * 32
        tally[...] = jnp.zeros_like(tally)
        for o in range(9):
            same = jnp.where(offset == o - HW, 1.0, 0.0)
            tally[pl.ds(o, 1), pl.ds(0, 32)] = jnp.sum(same, axis=0, keepdims=True)
        lt.start()

    def often(i, o):
        row = 16 * c + i
        return jnp.where(
            row < 32, count[o, row], count_next[o, jnp.maximum(row - 32, 0)]
        )

    rows = lax.broadcasted_iota(jnp.int32, (8, LEAF), 0)

    def factors(e):
        at = cols(e)
        pts = (px[:, at] - 0.5) * SCALE
        pts = jnp.concatenate([pts, jnp.zeros((5, LEAF), F32)], axis=0)
        high = pts.astype(BF16).astype(F32)
        low = (pts - high).astype(BF16).astype(F32)
        both = high + low
        norm = jnp.sum(both * both, axis=0, keepdims=True)
        n1 = norm.astype(BF16).astype(F32)
        n2 = (norm - n1).astype(BF16).astype(F32)
        n3 = (norm - n1 - n2).astype(BF16).astype(F32)
        norms = jnp.where(
            rows == 3, n1, jnp.where(rows == 4, n2, jnp.where(rows == 5, n3, 0.0))
        )
        ones = jnp.where((rows >= 3) & (rows <= 5), 1.0, 0.0)
        fa[:, at] = jnp.concatenate([high + norms, high + ones, low, low], axis=0).astype(BF16)
        fb[:, at] = jnp.concatenate(
            [ones - 2 * high, norms - 2 * low, -2 * high, -2 * low], axis=0
        ).astype(BF16)

    def kernel_unit(u):
        for h in range(2):
            q = 2 * u + h
            for b in range(HW + 1):
                kb[q, :, pl.ds(b * LEAF, LEAF)] = entries(
                    dot(fa[:, cols(q + HW)], fb[:, cols(q + HW + b)], 0, 0)
                )

    def near_main(i):
        e = i + HW
        mine = vx[:, cols(e)]
        total = None
        parts = []
        for o in range(HW + 1):
            block = kb[i, :, pl.ds(o * LEAF, LEAF)]
            term = dot(vx[:, cols(e + o)], block, 1, 1) * often(i, HW + o)
            total = term if total is None else total + term
            if o:
                parts.append(dot(mine, block, 1, 0) * often(i + o, HW - o))
        acc[:, cols(e, HW + 1)] += jnp.concatenate([total] + parts, axis=1)

    def joined(read, m):
        return jnp.concatenate(
            [jnp.concatenate([read(2 * j), read(2 * j + 1)], axis=1) for j in range(m)], axis=0
        )

    def upward(src, at, dst, to, m, weight):
        whole = dot(joined(lambda j: src[at + j], m), wup[weight]).astype(BF16)
        for j in range(m):
            dst[to + j] = whole[32 * j : 32 * j + 32]

    def levels(stage, weight):
        buf, size = stage[:2]
        at, m = 0, size
        while m > 2:
            upward(buf, at, buf, at + m, m // 2, weight)
            at, m, weight = at + m, m // 2, weight + 1
        return at, weight

    def merged(stage, weight):
        at, weight = levels(stage, weight)
        return dot(joined(lambda j: stage[0][at + j], 1), wup[weight]).astype(BF16)

    def depth(size):
        return (size - 1).bit_length()

    def enter():
        pl.semaphore_wait(barrier, 3 + c + (zn - 1) + (xn - 1) + (yn - 1))
        for copy in (sb, sv):
            copy.start()

        @pl.when(c == 0)
        def _():
            sp.start()
            st.start()

        sr.start()
        sl.start()
        weights()

    lanes = lax.broadcasted_iota(jnp.int32, (32, 128), 1) < 64

    def coefficients():
        lv.wait()
        sv.wait_recv()
        lb.wait()
        sb.wait_recv()
        lt.wait()

        @pl.loop(0, OWN, step=8)
        def _(i0):
            for k in range(8):
                i = i0 + k
                mine = bx[16 * c + i]
                full = dot(
                    vx[:, cols(i + HW)], jnp.concatenate([mine, mine], axis=0), 1, 1
                )
                dco[i] = full.astype(BF16)
                lev[i] = jnp.where(lanes, full[0:32], full[32:64]).astype(BF16)

        upward(lev, 0, lev, 16, 8, 0)
        upward(lev, 16, lev, 24, 4, 0)
        upward(lev, 24, lev, 28, 2, 0)
        whole = dot(joined(lambda j: lev[28 + j], 1), wup[0]).astype(BF16)
        lev[30] = whole
        pair[c] = whole
        sn.start()
        for copy in (sc, se0, se1, lf):
            copy.start()

    def z_stage():
        sn.wait_recv()
        zb[z] = dot(joined(lambda j: pair[j], 1), wup[0]).astype(BF16)
        ring_start(stages[0])

    def x_stage():
        ring_recv(stages[0])
        xb[x] = merged(stages[0], 1)
        ring_start(stages[1])

    def y_stage():
        ring_recv(stages[1])
        yb[y] = merged(stages[1], 1 + depth(zn))
        ring_start(stages[2])

    def rims():
        @pl.when(c == 1)
        def _():
            sp.wait_recv()
            for r in range(2):
                arrived(vx.at[pl.ds(0, 32), cols(20, 4)], 4 + r)
            st.wait_recv()
            lu.start()
            for e in range(4):
                factors(e + 20)
            lu.wait()

    def place(k):
        at = SCHEDULE[-1][k]
        for row in range(len(SCHEDULE) - 1):
            at = jnp.where(z == row, SCHEDULE[row][k], at)
        return at

    last = place(5)
    events = tuple(
        (place(k), event)
        for k, event in enumerate((enter, coefficients, z_stage, x_stage, y_stage))
    ) + ((last, rims), (last + 4, ss.start))

    lp.wait()

    @pl.loop(0, 20, step=4)
    def _(e):
        for k in range(4):
            factors(e + k + 4 - 4 * c)

    acc[...] = jnp.zeros_like(acc)
    fco[40] = jnp.zeros((32, 128), BF16)
    counts()

    @pl.loop(0, 16)
    def _(t):
        for when, event in events:
            pl.when(t == when)(event)

        kernels = (t < last + 2) | ((t >= last + 4) & (t < 10))

        @pl.when(kernels)
        def _():
            kernel_unit(jnp.where(t < last, t, jnp.where(t < last + 2, t - last + 6, t - 4)))

        @pl.when(jnp.logical_not(kernels))
        def _():
            i = 2 * jnp.where(t < last + 4, t - last + 4, t - 10)
            near_main(i)
            near_main(i + 1)

    ss.wait_recv()
    acc[:, cols(HW, HW)] += spill[...]
    so.start()
    ln.start()

    lf.wait()
    sc.wait_recv()
    for r in range(2):
        arrived(fco.at[pl.ds(0, HW)], 7 + r)
    lc.wait()
    pick0 = jnp.where(lanes, 1.0, 0.0).astype(BF16)
    pick1 = jnp.where(lanes, 0.0, 1.0).astype(BF16)

    @pl.loop(0, 32, step=4)
    def _(i0):
        for k in range(4):
            i = i0 + k
            used = far_count[i]
            at = [jnp.where(s < used, far_list[s, i] - d * 32 + HW, 40) for s in range(8)]
            coeffs = jnp.concatenate(
                [fco[at[2 * q]] * pick0 + fco[at[2 * q + 1]] * pick1 for q in range(4)], axis=1
            )
            yfar[i] = dot(coeffs, cv[i].reshape(512, 64))

    ring_recv(stages[2])
    levels(stages[2], 1 + depth(zn) + depth(xn))

    down = jnp.zeros((32, 128), BF16)
    u = upl - 1
    for buf, size, me, _, _, _ in reversed(stages):
        for step in range(depth(size) - 1, -1, -1):
            here = me // 2**step
            side = lax.rem(here, 2)
            sibling = buf[2 * size - 2 * (size >> step) + here + 1 - 2 * side]
            both = jnp.concatenate([sibling, down], axis=1)
            down = dot(both, wdn[2 * u + side]).astype(BF16)
            u -= 1

    whole = dot(down, wsel[...])
    for s in range(2):
        child = whole[:, 128 * s : 128 * s + 128]
        nodes[s] = jnp.where(lanes[0:16], child[0:16], child[16:32]).astype(BF16)
    at, m = 0, 2
    while m < OWN:
        whole = jnp.concatenate([nodes[at + j] for j in range(m)], axis=0)
        child = dot(whole, wld[...]).astype(BF16)
        for j in range(m):
            for s in range(2):
                nodes[at + m + 2 * j + s] = child[
                    16 * j : 16 * j + 16, 128 * s : 128 * s + 128
                ]
        at, m = at + m, 2 * m
    whole = jnp.concatenate([nodes[at + j] for j in range(OWN)], axis=0)
    for h in range(2):
        low = dot(whole, wleaf[h])
        for j in range(OWN):
            for s in range(2):
                ldown[2 * j + s, pl.ds(16 * h, 16), :] = low[
                    16 * j : 16 * j + 16, 128 * s : 128 * s + 128
                ]

    sl.wait_recv()
    ln.wait()
    so.wait_recv()

    @pl.loop(0, 32, step=8)
    def _(i0):
        for k in range(8):
            i = i0 + k
            leaf_local = (yfar[i] + ldown[i][:, 0:64]).astype(BF16)
            out[:, cols(i)] += dot(leaf_local, bx[i])

    for copy in (sv, sb, sl, sr, sc, se0, se1, sn, ss, so):
        copy.wait_send()

    @pl.when(c == 0)
    def _():
        sp.wait_send()
        st.wait_send()

    for stage in stages:

        @pl.loop(1, stage[1])
        def _(t):
            ring(stage, t).wait_send()


def solution(mesh):
    n = mesh.shape["leaf"]
    dims = (4, 4, 8) if n == 128 else (2, 2, n // 4)
    yn, xn, zn = dims
    upl = (n - 1).bit_length()
    hbm = pl.BlockSpec(memory_space=pltpu.HBM)
    vmem = pl.BlockSpec(memory_space=pltpu.VMEM)
    smem = pl.BlockSpec(memory_space=pltpu.SMEM)
    dma = pltpu.SemaphoreType.DMA

    def on_device(values, points, basis, near_list, far_list, *rest):
        return pl.pallas_call(
            functools.partial(kernel, dims),
            out_shape=pltpu.VMEM((32, 8192), F32),
            in_specs=[hbm, hbm, hbm, vmem, smem, smem, hbm, vmem, vmem, vmem],
            out_specs=vmem,
            scratch_shapes=[
                pltpu.VMEM((64, EXT * LEAF), BF16),
                pltpu.VMEM((3, EXT * LEAF), F32),
                pltpu.VMEM((32, EXT * LEAF), BF16),
                pltpu.VMEM((32, EXT * LEAF), BF16),
                pltpu.VMEM((32, 64, LEAF), BF16),
                pltpu.VMEM((32, 8, 64, 64), BF16),
                pltpu.VMEM((OWN, LEAF, (HW + 1) * LEAF), BF16),
                pltpu.VMEM((64, EXT * LEAF), F32),
                pltpu.VMEM((OWN, 64, 128), BF16),
                pltpu.VMEM((41, 32, 128), BF16),
                pltpu.VMEM((31, 32, 128), BF16),
                pltpu.VMEM((32, 32, 128), F32),
                pltpu.VMEM((32, 32, 64), F32),
                pltpu.VMEM((30, 16, 128), BF16),
                pltpu.VMEM((2, 32, 128), BF16),
                pltpu.VMEM((2 * zn, 32, 128), BF16),
                pltpu.VMEM((2 * xn, 32, 128), BF16),
                pltpu.VMEM((2 * yn, 32, 128), BF16),
                pltpu.VMEM((upl, 256, 128), BF16),
                pltpu.VMEM((2 * upl, 256, 128), BF16),
                pltpu.VMEM((128, 256), BF16),
                pltpu.VMEM((128, 256), BF16),
                pltpu.VMEM((2, 128, 256), BF16),
                pltpu.VMEM((16, 128), F32),
                pltpu.VMEM((16, 128), F32),
                pltpu.SMEM((16, 128), F32),
                pltpu.SMEM((16, 128), F32),
                pltpu.VMEM((64, HW * LEAF), F32),
                dma((8,)),
                dma((12,)),
                dma((13,)),
                dma((zn - 1,)),
                dma((zn - 1,)),
                dma((xn - 1,)),
                dma((xn - 1,)),
                dma((yn - 1,)),
                dma((yn - 1,)),
            ],
            compiler_params=pltpu.CompilerParams(
                collective_id=0, has_side_effects=True, vmem_limit_bytes=56 * 2**20
            ),
            name="h2_matvec",
        )(values, points, basis, near_list.T, far_list.T, *rest)

    placed = (
        P("rhs", "leaf"),
        P(None, "leaf"),
        P("leaf", "rhs", None),
        P("leaf", None),
        P("leaf", None),
        P("leaf"),
        P("leaf", None, None, None),
        P(),
        P(),
        P(),
    )
    return jax.shard_map(
        on_device, mesh=mesh, in_specs=placed, out_specs=P("rhs", "leaf"), check_vma=False
    )
```

time: 762 us -> 40.1 us (0.05)
  the two profiles are of different devices: /device:TPU:32 before, /device:TPU:1 now
where the time goes in v2:
time: 40.1 us; the launch traced here: 40 us
  Pallas kernels  39 us (97%)
  local copies, waits for them, and re-layouts  0.97 us (2%)
    pallas_call x1, Pallas kernels, on_device(): pl.pallas_call(functools.partial(kernel, dims), out_shape=pltpu.VMEM((32,...  39 us
    unnamed x1, local copies, waits for them, and re-layouts  0.97 us

profile of v2, /device:TPU:1, one launch (start us, length us, event | category | flops | bytes accessed | tf_op | source)
XLA Modules:
  0.0 40.0 jit_solution(16668625936812121382)
XLA Ops:
  0.0 39.0 %h2_matvec.1 = f32[32,8192]{1,0:T(8,128)S(1)} custom-call(bf16[32,8192]{1,0:T(8,128)(2,1)} %values.1, f32[3,8192]{1,0:T(4,128)} %points.1, bf16[32,32,256]{2,1,0:T(8,128)(2,1)} %basis.1, s32[9,32]{1,0:T(8,128)} %bitcast.2, s32[8,32]{1,0:T(8,128)} %bitcast.3, s32[32]{0:T(128)} %far_count.1, bf16[32,8,64,64]{3,2,1,0:T(8,128)(2,1)} %couple.1, ...), custom_call_target="tpu_custom_call" | custom-call | tf_op jit(solution)/shard_map/h2_matvec/pallas_call | solution.py:570
  39.0 1.0 %copy.12 = f32[32,8192]{1,0:T(8,128)} copy(f32[32,8192]{1,0:T(8,128)S(1)} %h2_matvec.1) | data formatting | bytes 2097152

commit v3 on v2

--- a/solution.py
+++ b/solution.py
@@ -22,11 +22,12 @@
 SOFT = SCALE * SCALE * SMOOTH * SMOOTH
 DEGREE = 4
 SCHEDULE = (
-    (5, 5, 8, 10, 14, 5),
-    (4, 5, 7, 10, 13, 4),
-    (4, 4, 6, 9, 12, 4),
-    (3, 3, 5, 8, 10, 3),
-    (2, 2, 4, 7, 9, 2),
+    (5, 0, 0, 5, 10, 0),
+    (4, 0, 0, 4, 10, 1),
+    (3, 0, 0, 4, 10, 1),
+    (3, 0, 0, 4, 10, 1),
+    (2, 0, 0, 4, 10, 1),
+    (1, 1, 1, 5, 10, 1),
 )
 
 
@@ -35,11 +36,11 @@
     series = np.polynomial.chebyshev.Chebyshev.fit(
         nodes, np.cos(2 * np.pi * np.sqrt(nodes)), DEGREE, domain=[0, 0.25]
     )
-    power = series.convert(kind=np.polynomial.Polynomial).coef
-    return [float(v) for v in power * SCALE / math.sqrt(9 * LEAF)]
+    return [float(v) for v in series.convert(kind=np.polynomial.Polynomial).coef]
 
 
 COSINE = cosine_fit()
+FACTOR = COSINE[DEGREE] * SCALE / math.sqrt(9 * LEAF)
 
 
 def entries(scaled):
@@ -47,9 +48,9 @@
     turns = scaled * lax.rsqrt(scaled)
     rest = turns - jnp.round(turns)
     square = rest * rest
-    poly = COSINE[DEGREE]
-    for power in range(DEGREE - 1, -1, -1):
-        poly = poly * square + COSINE[power]
+    poly = square + COSINE[DEGREE - 1] / COSINE[DEGREE]
+    for power in range(DEGREE - 2, -1, -1):
+        poly = poly * square + COSINE[power] / COSINE[DEGREE]
     return (poly * lax.rsqrt(scaled + SOFT)).astype(BF16)
 
 
@@ -103,7 +104,7 @@
     wup,
     wdn,
     wld,
-    wsel,
+    wroot,
     wleaf,
     tally,
     tally_next,
@@ -258,10 +259,11 @@
             wup[0, pl.ds(128 * s, 128), :] = diagonal(t)
             td = t.astype(F32).T
             wld[:, pl.ds(128 * s, 128)] = diagonal(td)
-            wsel[pl.ds(64 * c, 64), pl.ds(128 * s, 128)] = jnp.concatenate(
-                [td, td], axis=1
+            tf = t.astype(F32)
+            wroot[pl.ds(128 * s + 64 * c, 64), :] = jnp.concatenate(
+                [tf, tf], axis=1
             ).astype(BF16)
-            wsel[pl.ds(64 * p, 64), pl.ds(128 * s, 128)] = none
+            wroot[pl.ds(128 * s + 64 * p, 64), :] = none
             wide = jnp.concatenate([td, zero], axis=1).astype(BF16)
             wleaf[0, pl.ds(0, 64), pl.ds(128 * s, 128)] = wide
             wleaf[0, pl.ds(64, 64), pl.ds(128 * s, 128)] = none
@@ -280,7 +282,7 @@
         offset = near_list[...] - leaf - d * 32
         tally[...] = jnp.zeros_like(tally)
         for o in range(9):
-            same = jnp.where(offset == o - HW, 1.0, 0.0)
+            same = jnp.where(offset == o - HW, FACTOR, 0.0)
             tally[pl.ds(o, 1), pl.ds(0, 32)] = jnp.sum(same, axis=0, keepdims=True)
         lt.start()
 
@@ -312,13 +314,16 @@
             [ones - 2 * high, norms - 2 * low, -2 * high, -2 * low], axis=0
         ).astype(BF16)
 
-    def kernel_unit(u):
-        for h in range(2):
-            q = 2 * u + h
-            for b in range(HW + 1):
-                kb[q, :, pl.ds(b * LEAF, LEAF)] = entries(
-                    dot(fa[:, cols(q + HW)], fb[:, cols(q + HW + b)], 0, 0)
-                )
+    def kernel_row(q):
+        left = fa[:, cols(q + HW)]
+        own_right = fb[:, cols(q + HW)]
+        top = entries(dot(left[:, 0:128], own_right, 0, 0))
+        low = entries(dot(left[:, 128:256], own_right[:, 128:256], 0, 0))
+        kb[q, pl.ds(0, 128), pl.ds(0, LEAF)] = top
+        kb[q, pl.ds(128, 128), pl.ds(128, 128)] = low
+        kb[q, pl.ds(128, 128), pl.ds(0, 128)] = top[:, 128:256].T
+        for b in range(1, HW + 1):
+            kb[q, :, pl.ds(b * LEAF, LEAF)] = entries(dot(left, fb[:, cols(q + HW + b)], 0, 0))
 
     def near_main(i):
         e = i + HW
@@ -339,9 +344,10 @@
         )
 
     def upward(src, at, dst, to, m, weight):
+        high = src.shape[1]
         whole = dot(joined(lambda j: src[at + j], m), wup[weight]).astype(BF16)
         for j in range(m):
-            dst[to + j] = whole[32 * j : 32 * j + 32]
+            dst[to + j] = whole[high * j : high * j + high]
 
     def levels(stage, weight):
         buf, size = stage[:2]
@@ -404,7 +410,8 @@
 
     def z_stage():
         sn.wait_recv()
-        zb[z] = dot(joined(lambda j: pair[j], 1), wup[0]).astype(BF16)
+        root = dot(joined(lambda j: pair[j], 1), wroot[...])
+        zb[z] = jnp.where(lanes[0:16], root[0:16], root[16:32]).astype(BF16)
         ring_start(stages[0])
 
     def x_stage():
@@ -431,15 +438,16 @@
 
     def place(k):
         at = SCHEDULE[-1][k]
-        for row in range(len(SCHEDULE) - 1):
-            at = jnp.where(z == row, SCHEDULE[row][k], at)
-        return at
-
+        for row in range(1, len(SCHEDULE) - 1):
+            at = jnp.where(z == row - 1, SCHEDULE[row][k], at)
+        return jnp.where(d == 0, SCHEDULE[0][k], at)
+
+    ahead = place(0)
     last = place(5)
     events = tuple(
-        (place(k), event)
-        for k, event in enumerate((enter, coefficients, z_stage, x_stage, y_stage))
-    ) + ((last, rims), (last + 4, ss.start))
+        (place(k + 1), event)
+        for k, event in enumerate((coefficients, z_stage, x_stage, y_stage))
+    ) + ((last, rims), (last + HW + 2, ss.start))
 
     lp.wait()
 
@@ -452,20 +460,29 @@
     fco[40] = jnp.zeros((32, 128), BF16)
     counts()
 
-    @pl.loop(0, 16)
+    @pl.loop(0, ahead)
+    def _(t):
+        kernel_row(2 * t)
+        kernel_row(2 * t + 1)
+
+    enter()
+
+    @pl.loop(0, 24 - 2 * ahead)
     def _(t):
         for when, event in events:
             pl.when(t == when)(event)
-
-        kernels = (t < last + 2) | ((t >= last + 4) & (t < 10))
+        left = 18 - 2 * ahead
+        here = t - last
+        kernels = (here < HW) | ((here >= HW + 2) & (t < left))
 
         @pl.when(kernels)
         def _():
-            kernel_unit(jnp.where(t < last, t, jnp.where(t < last + 2, t - last + 6, t - 4)))
+            row = jnp.where(here < HW, here + 12, 2 * ahead + t - HW - 2)
+            kernel_row(jnp.where(here < 0, 2 * ahead + t, row))
 
         @pl.when(jnp.logical_not(kernels))
         def _():
-            i = 2 * jnp.where(t < last + 4, t - last + 4, t - 10)
+            i = 2 * jnp.where(t < left, here + 2, t - left)
             near_main(i)
             near_main(i + 1)
 
@@ -496,7 +513,7 @@
     ring_recv(stages[2])
     levels(stages[2], 1 + depth(zn) + depth(xn))
 
-    down = jnp.zeros((32, 128), BF16)
+    down = jnp.zeros((16, 128), BF16)
     u = upl - 1
     for buf, size, me, _, _, _ in reversed(stages):
         for step in range(depth(size) - 1, -1, -1):
@@ -507,11 +524,8 @@
             down = dot(both, wdn[2 * u + side]).astype(BF16)
             u -= 1
 
-    whole = dot(down, wsel[...])
-    for s in range(2):
-        child = whole[:, 128 * s : 128 * s + 128]
-        nodes[s] = jnp.where(lanes[0:16], child[0:16], child[16:32]).astype(BF16)
-    at, m = 0, 2
+    nodes[0] = down
+    at, m = 0, 1
     while m < OWN:
         whole = jnp.concatenate([nodes[at + j] for j in range(m)], axis=0)
         child = dot(whole, wld[...]).astype(BF16)
@@ -586,15 +600,15 @@
                 pltpu.VMEM((31, 32, 128), BF16),
                 pltpu.VMEM((32, 32, 128), F32),
                 pltpu.VMEM((32, 32, 64), F32),
-                pltpu.VMEM((30, 16, 128), BF16),
+                pltpu.VMEM((31, 16, 128), BF16),
                 pltpu.VMEM((2, 32, 128), BF16),
-                pltpu.VMEM((2 * zn, 32, 128), BF16),
-                pltpu.VMEM((2 * xn, 32, 128), BF16),
-                pltpu.VMEM((2 * yn, 32, 128), BF16),
+                pltpu.VMEM((2 * zn, 16, 128), BF16),
+                pltpu.VMEM((2 * xn, 16, 128), BF16),
+                pltpu.VMEM((2 * yn, 16, 128), BF16),
                 pltpu.VMEM((upl, 256, 128), BF16),
                 pltpu.VMEM((2 * upl, 256, 128), BF16),
                 pltpu.VMEM((128, 256), BF16),
-                pltpu.VMEM((128, 256), BF16),
+                pltpu.VMEM((256, 128), BF16),
                 pltpu.VMEM((2, 128, 256), BF16),
                 pltpu.VMEM((16, 128), F32),
                 pltpu.VMEM((16, 128), F32),

time: 40.1 us -> 38 us (0.948)
  Pallas kernels: 39 us -> 36.9 us
    pallas_call x1, Pallas kernels: 39 us -> 36.9 us  [on_device(): pl.pallas_call(functools.partial(kernel, dims), out_shape=pltpu.VMEM((32,...]
where the time goes in v3:
time: 38 us; the launch traced here: 37.9 us
  Pallas kernels  36.9 us (97%)
  local copies, waits for them, and re-layouts  0.97 us (3%)
    pallas_call x1, Pallas kernels, on_device(): pl.pallas_call(functools.partial(kernel, dims), out_shape=pltpu.VMEM((32,...  36.9 us
    unnamed x1, local copies, waits for them, and re-layouts  0.97 us

profile of v3, /device:TPU:1, one launch (start us, length us, event | category | flops | bytes accessed | tf_op | source)
XLA Modules:
  0.0 37.9 jit_solution(3211140380983875306)
XLA Ops:
  0.0 36.9 %h2_matvec.1 = f32[32,8192]{1,0:T(8,128)S(1)} custom-call(bf16[32,8192]{1,0:T(8,128)(2,1)} %values.1, f32[3,8192]{1,0:T(4,128)} %points.1, bf16[32,32,256]{2,1,0:T(8,128)(2,1)} %basis.1, s32[9,32]{1,0:T(8,128)} %bitcast.2, s32[8,32]{1,0:T(8,128)} %bitcast.3, s32[32]{0:T(128)} %far_count.1, bf16[32,8,64,64]{3,2,1,0:T(8,128)(2,1)} %couple.1, ...), custom_call_target="tpu_custom_call" | custom-call | tf_op jit(solution)/shard_map/h2_matvec/pallas_call | solution.py:584
  36.9 1.0 %copy.12 = f32[32,8192]{1,0:T(8,128)} copy(f32[32,8192]{1,0:T(8,128)S(1)} %h2_matvec.1) | data formatting | bytes 2097152

commit v4 on v3

--- a/solution.py
+++ b/solution.py
@@ -22,12 +22,12 @@
 SOFT = SCALE * SCALE * SMOOTH * SMOOTH
 DEGREE = 4
 SCHEDULE = (
-    (5, 0, 0, 5, 10, 0),
-    (4, 0, 0, 4, 10, 1),
-    (3, 0, 0, 4, 10, 1),
-    (3, 0, 0, 4, 10, 1),
-    (2, 0, 0, 4, 10, 1),
-    (1, 1, 1, 5, 10, 1),
+    (4, 0, 0, 4, 9, 0),
+    (3, 0, 0, 4, 9, 1),
+    (2, 0, 0, 4, 9, 1),
+    (2, 0, 0, 4, 9, 1),
+    (1, 0, 0, 4, 9, 1),
+    (1, 0, 0, 5, 9, 1),
 )
 
 
@@ -447,7 +447,7 @@
     events = tuple(
         (place(k + 1), event)
         for k, event in enumerate((coefficients, z_stage, x_stage, y_stage))
-    ) + ((last, rims), (last + HW + 2, ss.start))
+    ) + ((last, rims), (last + HW + 1, ss.start))
 
     lp.wait()
 
@@ -467,24 +467,24 @@
 
     enter()
 
-    @pl.loop(0, 24 - 2 * ahead)
+    @pl.loop(0, 20 - 2 * ahead)
     def _(t):
         for when, event in events:
             pl.when(t == when)(event)
-        left = 18 - 2 * ahead
+        left = 17 - 2 * ahead
         here = t - last
-        kernels = (here < HW) | ((here >= HW + 2) & (t < left))
+        kernels = (here < HW) | ((here > HW) & (t < left))
 
         @pl.when(kernels)
         def _():
-            row = jnp.where(here < HW, here + 12, 2 * ahead + t - HW - 2)
+            row = jnp.where(here < HW, here + 12, 2 * ahead + t - HW - 1)
             kernel_row(jnp.where(here < 0, 2 * ahead + t, row))
 
         @pl.when(jnp.logical_not(kernels))
         def _():
-            i = 2 * jnp.where(t < left, here + 2, t - left)
-            near_main(i)
-            near_main(i + 1)
+            i = 4 * jnp.where(t < left, 3, t - left)
+            for k in range(4):
+                near_main(i + k)
 
     ss.wait_recv()
     acc[:, cols(HW, HW)] += spill[...]
@@ -499,18 +499,16 @@
     pick0 = jnp.where(lanes, 1.0, 0.0).astype(BF16)
     pick1 = jnp.where(lanes, 0.0, 1.0).astype(BF16)
 
-    @pl.loop(0, 32, step=4)
-    def _(i0):
-        for k in range(4):
-            i = i0 + k
-            used = far_count[i]
-            at = [jnp.where(s < used, far_list[s, i] - d * 32 + HW, 40) for s in range(8)]
-            coeffs = jnp.concatenate(
-                [fco[at[2 * q]] * pick0 + fco[at[2 * q + 1]] * pick1 for q in range(4)], axis=1
-            )
-            yfar[i] = dot(coeffs, cv[i].reshape(512, 64))
-
     ring_recv(stages[2])
+
+    for i in range(32):
+        used = far_count[i]
+        at = [jnp.where(s < used, far_list[s, i] - d * 32 + HW, 40) for s in range(8)]
+        coeffs = jnp.concatenate(
+            [fco[at[2 * q]] * pick0 + fco[at[2 * q + 1]] * pick1 for q in range(4)], axis=1
+        )
+        yfar[i] = dot(coeffs, cv[i].reshape(512, 64))
+
     levels(stages[2], 1 + depth(zn) + depth(xn))
 
     down = jnp.zeros((16, 128), BF16)

time: 38 us -> 37 us (0.974)
  Pallas kernels: 36.9 us -> 35.9 us
    pallas_call x1, Pallas kernels: 36.9 us -> 35.9 us  [on_device(): pl.pallas_call(functools.partial(kernel, dims), out_shape=pltpu.VMEM((32,...]
where the time goes in v4:
time: 37 us; the launch traced here: 36.9 us
  Pallas kernels  35.9 us (97%)
  local copies, waits for them, and re-layouts  0.97 us (3%)
    pallas_call x1, Pallas kernels, on_device(): pl.pallas_call(functools.partial(kernel, dims), out_shape=pltpu.VMEM((32,...  35.9 us
    unnamed x1, local copies, waits for them, and re-layouts  0.97 us

profile of v4, /device:TPU:1, one launch (start us, length us, event | category | flops | bytes accessed | tf_op | source)
XLA Modules:
  0.0 36.9 jit_solution(3576626518214602306)
XLA Ops:
  0.0 35.9 %h2_matvec.1 = f32[32,8192]{1,0:T(8,128)S(1)} custom-call(bf16[32,8192]{1,0:T(8,128)(2,1)} %values.1, f32[3,8192]{1,0:T(4,128)} %points.1, bf16[32,32,256]{2,1,0:T(8,128)(2,1)} %basis.1, s32[9,32]{1,0:T(8,128)} %bitcast.2, s32[8,32]{1,0:T(8,128)} %bitcast.3, s32[32]{0:T(128)} %far_count.1, bf16[32,8,64,64]{3,2,1,0:T(8,128)(2,1)} %couple.1, ...), custom_call_target="tpu_custom_call" | custom-call | tf_op jit(solution)/shard_map/h2_matvec/pallas_call | solution.py:582
  35.9 1.0 %copy.12 = f32[32,8192]{1,0:T(8,128)} copy(f32[32,8192]{1,0:T(8,128)S(1)} %h2_matvec.1) | data formatting | bytes 2097152

commit v5 on v4

--- a/solution.py
+++ b/solution.py
@@ -387,8 +387,7 @@
         sb.wait_recv()
         lt.wait()
 
-        @pl.loop(0, OWN, step=8)
-        def _(i0):
+        for i0 in range(0, OWN, 8):
             for k in range(8):
                 i = i0 + k
                 mine = bx[16 * c + i]
@@ -442,12 +441,18 @@
             at = jnp.where(z == row - 1, SCHEDULE[row][k], at)
         return jnp.where(d == 0, SCHEDULE[0][k], at)
 
+    sends = (d < n - 1) | (c == 0)
+    takes = (d > 0) | (c == 1)
+
+    def spill_start():
+        pl.when(sends)(ss.start)
+
     ahead = place(0)
     last = place(5)
     events = tuple(
         (place(k + 1), event)
         for k, event in enumerate((coefficients, z_stage, x_stage, y_stage))
-    ) + ((last, rims), (last + HW + 1, ss.start))
+    ) + ((last, rims), (last + HW + 1, spill_start))
 
     lp.wait()
 
@@ -486,8 +491,11 @@
             for k in range(4):
                 near_main(i + k)
 
-    ss.wait_recv()
-    acc[:, cols(HW, HW)] += spill[...]
+    @pl.when(takes)
+    def _():
+        ss.wait_recv()
+        acc[:, cols(HW, HW)] += spill[...]
+
     so.start()
     ln.start()
 
@@ -553,8 +561,9 @@
             leaf_local = (yfar[i] + ldown[i][:, 0:64]).astype(BF16)
             out[:, cols(i)] += dot(leaf_local, bx[i])
 
-    for copy in (sv, sb, sl, sr, sc, se0, se1, sn, ss, so):
+    for copy in (sv, sb, sl, sr, sc, se0, se1, sn, so):
         copy.wait_send()
+    pl.when(sends)(ss.wait_send)
 
     @pl.when(c == 0)
     def _():

time: 37 us -> 36.5 us (0.986)
  the two profiles are of different devices: /device:TPU:1 before, /device:TPU:96 now
where the time goes in v5:
time: 36.5 us
  Pallas kernels  35.5 us (97%)
  local copies, waits for them, and re-layouts  0.97 us (3%)
    pallas_call x1, Pallas kernels, on_device(): pl.pallas_call(functools.partial(kernel, dims), out_shape=pltpu.VMEM((32,...  35.5 us
    unnamed x1, local copies, waits for them, and re-layouts  0.97 us

profile of v5, /device:TPU:96, one launch (start us, length us, event | category | flops | bytes accessed | tf_op | source)
XLA Modules:
  0.0 36.5 jit_solution(3804319354466707700)
XLA Ops:
  0.0 35.5 %h2_matvec.1 = f32[32,8192]{1,0:T(8,128)S(1)} custom-call(bf16[32,8192]{1,0:T(8,128)(2,1)} %values.1, f32[3,8192]{1,0:T(4,128)} %points.1, bf16[32,32,256]{2,1,0:T(8,128)(2,1)} %basis.1, s32[9,32]{1,0:T(8,128)} %bitcast.2, s32[8,32]{1,0:T(8,128)} %bitcast.3, s32[32]{0:T(128)} %far_count.1, bf16[32,8,64,64]{3,2,1,0:T(8,128)(2,1)} %couple.1, ...), custom_call_target="tpu_custom_call" | custom-call | tf_op jit(solution)/shard_map/h2_matvec/pallas_call | solution.py:591
  35.5 1.0 %copy.12 = f32[32,8192]{1,0:T(8,128)} copy(f32[32,8192]{1,0:T(8,128)S(1)} %h2_matvec.1) | data formatting | bytes 2097152
